TPU v7x, 512 devices: a whole 4x8x8 slice. The times are simulated.
512 devices in a mesh: seq: 64 (over x, z, core), head: 8 (over y).
Axes of the slice: x: 4, y: 8, z: 8, core: 2. Of those that a mesh axis runs over, the one named last changes fastest.
Arguments:
- queries: bfloat16 [32768, 2048], P(('seq', 'head')), may hold values from -6 to 6
- keys: bfloat16 [32768, 512], P(('seq', 'head')), may hold values from -6 to 6
- values: bfloat16 [32768, 512], P(('seq', 'head')), may hold values from -6 to 6
- vertical: int32 [16, 64], replicated, may hold values from 0 to 511, as said below
- offsets: int32 [16, 5], replicated, may hold values from 0 to 7, as said below
Outputs:
- attended: bfloat16 [32768, 2048], P(('seq', 'head'))
Inputs may be any that keep to these rules, and one draw needn't show every extreme that they name: `vertical`: entry [h, s + i], for i below 1, is a block of segment s, from s * 8 to (s + 1) * 8 - 1; the blocks of one head in one segment are distinct. The 5 offsets of one head are distinct and include 0 and 7.
All inputs are finite; a program needn't handle non-finite values.
Results may differ from a plain program's by a relative error of at most 0.0032.
Values may be sent and summed in bfloat16 or wider, within the bound.
A program may use at most 64 MiB of HBM per device.

v0:
```python
import jax
import jax.numpy as jnp
from jax import lax
from jax.sharding import PartitionSpec as P

HEADS = 16
KV_HEADS = 4
HDIM = 128
BLOCK = 64
VPS = 1


def passed_along(block, axis, distance):
    devices = range(lax.axis_size(axis))
    route = [(i - distance, i) for i in devices if i - distance in devices]
    return lax.ppermute(block, axis, route)


def attend_head(
    head_queries, band_keys, band_values, vert_keys, vert_values, vert_ids, slash_ids, first_block
):
    scale = HDIM ** (-0.5)
    seg_rows = head_queries.shape[0]
    span_tile_count = seg_rows // BLOCK
    row_count = min(512, seg_rows)
    row_blocks = row_count // BLOCK
    flat_keys = vert_keys.reshape(-1, HDIM)
    flat_values = vert_values.reshape(-1, HDIM)
    position = jnp.arange(BLOCK)
    causal = position[None, :] <= position[:, None]
    global_blocks = first_block + 0 // BLOCK + jnp.arange(row_blocks)
    distance = global_blocks[:, None] - vert_ids[None, :]
    on_slash = jnp.any(distance[:, :, None] == slash_ids[None, None, :], axis=2)
    vert_keep = (distance > 0) & jnp.logical_not(on_slash)
    vert_scores = jnp.dot(head_queries, flat_keys.T, preferred_element_type=jnp.float32) * scale
    vert_scores = vert_scores.reshape(row_blocks, BLOCK, -1, BLOCK)
    vert_scores = jnp.where(vert_keep[:, None, :, None], vert_scores, -jnp.inf)

    def band_slice(offset_value):
        begin = (span_tile_count - offset_value) * BLOCK + 0
        return (
            lax.dynamic_slice_in_dim(band_keys, begin, row_count, 0),
            lax.dynamic_slice_in_dim(band_values, begin, row_count, 0),
        )

    slant_band_indices, diagonal_values = jax.vmap(band_slice)(slash_ids)
    slant_band_indices = slant_band_indices.reshape(-1, row_blocks, BLOCK, HDIM)
    diagonal_values = diagonal_values.reshape(-1, row_blocks, BLOCK, HDIM)
    probe_partition_plan = head_queries.reshape(row_blocks, BLOCK, HDIM)
    slash_scores = (
        jnp.einsum(
            "sqe,vsae->sqva",
            probe_partition_plan,
            slant_band_indices,
            preferred_element_type=jnp.float32,
        )
        * scale
    )
    source_ok = global_blocks[:, None] - slash_ids[None, :] >= 0
    allowed = source_ok[:, None, :, None] & (
        (slash_ids[None, None, :, None] != 0) | causal[None, :, None, :]
    )
    slash_scores = jnp.where(allowed, slash_scores, -jnp.inf)
    top = jnp.maximum(jnp.max(vert_scores, axis=(2, 3)), jnp.max(slash_scores, axis=(2, 3)))
    vert_weights = jnp.exp(vert_scores - top[:, :, None, None])
    slash_weights = jnp.exp(slash_scores - top[:, :, None, None])
    total = jnp.sum(vert_weights, axis=(2, 3)) + jnp.sum(slash_weights, axis=(2, 3))
    vert_round = vert_weights.astype(jnp.bfloat16).reshape(row_count, -1)
    diagonal_rounded = slash_weights.astype(jnp.bfloat16)
    output = jnp.dot(vert_round, flat_values, preferred_element_type=jnp.float32).reshape(
        row_blocks, BLOCK, HDIM
    )
    output = output + jnp.einsum(
        "pvcg,cpgw->pvw", diagonal_rounded, diagonal_values, preferred_element_type=jnp.float32
    )
    pieces = (output / total[:, :, None]).reshape(row_count, HDIM).astype(jnp.bfloat16)
    return pieces


def body(queries, keys, values, vertical, offsets):
    number_of_attenders = lax.axis_size("head")
    per_device = HEADS // number_of_attenders
    group = HEADS // KV_HEADS
    head_index = lax.axis_index("head")
    seg_index = lax.axis_index("seq")
    tok_rows = queries.shape[0]
    query_head_group = queries.reshape(tok_rows, HEADS, HDIM)
    nearby_probe_vectors = lax.all_to_all(
        query_head_group, "head", split_axis=1, concat_axis=0, tiled=True
    )
    all_keys, all_values = (
        lax.all_gather(keys, "head", axis=0, tiled=True),
        lax.all_gather(values, "head", axis=0, tiled=True),
    )
    seg_rows = all_keys.shape[0]
    kv_local = max(1, per_device // group)
    kv_first = head_index * per_device // group
    nearby_lookup_vectors = lax.dynamic_slice_in_dim(
        all_keys.reshape(seg_rows, KV_HEADS, HDIM), kv_first, kv_local, 1
    )
    local_values = lax.dynamic_slice_in_dim(
        all_values.reshape(seg_rows, KV_HEADS, HDIM), kv_first, kv_local, 1
    )
    prior_keys, prior_values = passed_along((nearby_lookup_vectors, local_values), "seq", 1)
    kv_of = [member // group for member in range(per_device)]
    seg_rows = nearby_probe_vectors.shape[0]
    span_tile_count = seg_rows // BLOCK
    vert_heads = lax.dynamic_slice_in_dim(vertical, head_index * per_device, per_device, 0)
    slash_heads = lax.dynamic_slice_in_dim(offsets, head_index * per_device, per_device, 0)
    own_blocks = (
        lax.dynamic_slice_in_dim(vert_heads, seg_index * VPS, VPS, 1) - seg_index * span_tile_count
    )
    key_grid = nearby_lookup_vectors.reshape(span_tile_count, BLOCK, -1, HDIM)
    value_grid = local_values.reshape(span_tile_count, BLOCK, -1, HDIM)
    picked_keys = []
    picked_values = []
    for member in range(per_device):
        row_keys = [
            lax.dynamic_index_in_dim(
                key_grid[:, :, kv_of[member]], own_blocks[member, 0], 0, keepdims=False
            )
        ]
        row_values = [
            lax.dynamic_index_in_dim(
                value_grid[:, :, kv_of[member]], own_blocks[member, 0], 0, keepdims=False
            )
        ]
        picked_keys.append(jnp.stack(row_keys, axis=0))
        picked_values.append(jnp.stack(row_values, axis=0))
    picked_keys = jnp.stack(picked_keys, axis=0)
    picked_values = jnp.stack(picked_values, axis=0)
    vert_keys, vert_values = (
        lax.all_gather(picked_keys, "seq", axis=1, tiled=True),
        lax.all_gather(picked_values, "seq", axis=1, tiled=True),
    )
    first_block = seg_index * span_tile_count
    outputs = []
    for member in range(per_device):
        band_keys = jnp.concatenate(
            [prior_keys[:, kv_of[member]], nearby_lookup_vectors[:, kv_of[member]]], axis=0
        )
        band_values = jnp.concatenate(
            [prior_values[:, kv_of[member]], local_values[:, kv_of[member]]], axis=0
        )
        outputs.append(
            attend_head(
                nearby_probe_vectors[:, member],
                band_keys,
                band_values,
                vert_keys[member],
                vert_values[member],
                vert_heads[member],
                slash_heads[member],
                first_block,
            )
        )
    piled_matrix = jnp.stack(outputs, axis=1)
    final_outcome = lax.all_to_all(piled_matrix, "head", split_axis=0, concat_axis=1, tiled=True)
    return final_outcome.reshape(tok_rows, HEADS * HDIM)


def solution(mesh):
    placed = (
        P(("seq", "head"), None),
        P(("seq", "head"), None),
        P(("seq", "head"), None),
        P(),
        P(),
    )
    return jax.shard_map(
        body, mesh=mesh, in_specs=placed, out_specs=P(("seq", "head"), None), check_vma=False
    )
```

profile of v0, /device:TPU:1, one launch (start us, length us, event | category | flops | bytes accessed | tf_op | source)
XLA Modules:
  0.0 287.9 jit_solution(16816474941296417499)
XLA Ops:
  6.5 0.8 dynamic-slice_subtract_fusion
  10.5 21.9 %all_gather.12 = bf16[512,512]{1,0:T(8,128)(2,1)S(1)} all-gather(bf16[64,512]{1,0:T(8,128)(2,1)} %param.6), channel_id=1, replica_groups=mesh['seq'=64,'head'=8] {'head'}, dimensions={0}, use_global_device_ids=true | all-gather | bytes 589824 | tf_op jit(solution)/shard_map/all_gather | solution.py:92
  32.7 20.0 %all_gather.14 = bf16[512,512]{1,0:T(8,128)(2,1)S(1)} all-gather(bf16[64,512]{1,0:T(8,128)(2,1)} %param.7), channel_id=1, replica_groups=mesh['seq'=64,'head'=8] {'head'}, dimensions={0}, use_global_device_ids=true | all-gather | bytes 589824 | tf_op jit(solution)/shard_map/all_gather | solution.py:93
  52.9 0.7 constant_dynamic-slice_fusion.4
  53.6 1.0 copy.88
  56.0 0.6 pad_maximum_fusion.3
  56.7 16.2 %collective-permute-start = (bf16[512,1,128]{0,2,1:T(8,128)(2,1)S(1)}, bf16[512,1,128]{0,2,1:T(8,128)(2,1)S(1)}, u32[]{:S(2)}, u32[]{:S(2)}) collective-permute-start(bf16[512,1,128]{0,2,1:T(8,128)(2,1)S(1)} %constant_dynamic-slice_fusion.5), channel_id=1, source_target_pairs={{0,8},{8,16},{16,24},{24,32},{32,40},{40,48},{48,56},{56,64},{64,7... | collective-permute-start | bytes 393224 | tf_op jit(solution)/shard_map/ppermute | solution.py:16
  72.9 1.9 collective-permute-start.1
  74.9 0.8 copy_bitcast_fusion
  75.6 5.2 %all-to-all-start = ((bf16[64,16,128]{2,0,1:T(8,128)(2,1)}), bf16[64,16,128]{2,0,1:T(8,128)(2,1)}, u32[]{:S(2)}, u32[]{:S(2)}) async-start(bf16[64,16,128]{2,0,1:T(8,128)(2,1)} %copy_bitcast_fusion), calls=%async_computation | async-start | bytes 524288 | tf_op jit(solution)/shard_map/all_to_all | solution.py:88
  80.9 0.6 pad_maximum_fusion.4
  81.6 0.7 constant_dynamic-slice_fusion.7
  82.6 0.7 subtract_compare_fusion.1
  83.5 0.7 broadcast_or_fusion.1
  84.3 3.1 %broadcast_in_dim.31 = pred[8,64,64,64]{3,2,1,0:T(32,128)(4,1)} broadcast(pred[8,64]{1,0:T(8,128)(4,1)S(1)} %get-tuple-element.174), dimensions={0,2} | broadcast | bytes 2097664 | tf_op jit(solution)/shard_map/jit(_where)/broadcast_in_dim | solution.py:37
  87.4 12.0 %broadcast_in_dim.32 = pred[512,4096]{1,0:T(32,128)(4,1)} reshape(pred[8,64,64,64]{3,2,1,0:T(32,128)(4,1)} %broadcast_in_dim.31) | data formatting | bytes 4194304 | tf_op jit(solution)/shard_map/jit(_where)/broadcast_in_dim | solution.py:37
  99.4 3.1 %broadcast_in_dim.27 = pred[8,64,64,64]{3,2,1,0:T(32,128)(4,1)} broadcast(pred[8,64]{1,0:T(8,128)(4,1)S(1)} %get-tuple-element.173), dimensions={0,2} | broadcast | bytes 2097664 | tf_op jit(solution)/shard_map/jit(_where)/broadcast_in_dim | solution.py:37
  102.5 11.3 %broadcast_in_dim.28 = pred[512,4096]{1,0:T(32,128)(4,1)S(1)} reshape(pred[8,64,64,64]{3,2,1,0:T(32,128)(4,1)} %broadcast_in_dim.27) | data formatting | bytes 4194304 | tf_op jit(solution)/shard_map/jit(_where)/broadcast_in_dim | solution.py:37
  113.8 0.7 fusion.44
  114.8 5.9 %while.6 = (s32[]{:T(128)}, bf16[1024,128]{1,0:T(8,128)(2,1)S(1)}, s32[5,2]{0,1:T(2,128)S(1)}, bf16[5,512,128]{2,1,0:T(8,128)(2,1)S(1)}, s32[]{:T(128)}) while((s32[]{:T(128)}, bf16[1024,128]{1,0:T(8,128)(2,1)S(1)}, s32[5,2]{0,1:T(2,128)S(1)}, bf16[5,512,128]{2,1,0:T(8,128)(2,1)S(1)}, s32[]{:T(128)}) %tuple.94), condition=%wide.while_cond.2, body=%wide.while_body.2.sunk | while | flops 2 | bytes 262249 | solution.py:42
  115.3 0.6 bitcast_dynamic-update-slice_fusion.10
  116.5 0.6 bitcast_dynamic-update-slice_fusion.10
  117.7 0.6 bitcast_dynamic-update-slice_fusion.10
  118.9 0.6 bitcast_dynamic-update-slice_fusion.10
  120.7 0.8 copy-done.6
  121.5 0.9 pad_maximum_fusion.1
  122.7 7.1 %while.7 = (s32[]{:T(128)}, bf16[1024,128]{1,0:T(8,128)(2,1)S(1)}, s32[5,2]{0,1:T(2,128)S(1)}, bf16[5,512,128]{2,1,0:T(8,128)(2,1)S(1)}, s32[]{:T(128)}) while((s32[]{:T(128)}, bf16[1024,128]{1,0:T(8,128)(2,1)S(1)}, s32[5,2]{0,1:T(2,128)S(1)}, bf16[5,512,128]{2,1,0:T(8,128)(2,1)S(1)}, s32[]{:T(128)}) %tuple.113), condition=%wide.while_cond.3, body=%wide.while_body.3.sunk | while | flops 2 | bytes 262249 | solution.py:43
  123.4 0.7 bitcast_dynamic-update-slice_fusion.11
  124.8 0.7 bitcast_dynamic-update-slice_fusion.11
  126.3 0.7 bitcast_dynamic-update-slice_fusion.11
  127.7 0.7 bitcast_dynamic-update-slice_fusion.11
  129.1 0.7 bitcast_dynamic-update-slice_fusion.11
  129.9 1.0 broadcast.294.clone.2
  130.9 10.2 %while.4 = (s32[]{:T(128)}, bf16[1024,128]{1,0:T(8,128)(2,1)S(1)}, s32[5,2]{0,1:T(2,128)S(1)}, bf16[5,512,128]{2,1,0:T(8,128)(2,1)}, s32[]{:T(128)}) while((s32[]{:T(128)}, bf16[1024,128]{1,0:T(8,128)(2,1)S(1)}, s32[5,2]{0,1:T(2,128)S(1)}, bf16[5,512,128]{2,1,0:T(8,128)(2,1)}, s32[]{:T(128)}) %tuple.110), condition=%wide.while_cond, body=%wide.while_body.sunk | while | flops 2 | bytes 262757 | solution.py:42
  131.6 1.4 bitcast_dynamic-update-slice_fusion.8
  133.6 1.4 bitcast_dynamic-update-slice_fusion.8
  135.6 1.4 bitcast_dynamic-update-slice_fusion.8
  137.7 1.4 bitcast_dynamic-update-slice_fusion.8
  139.7 1.4 bitcast_dynamic-update-slice_fusion.8
  141.2 7.1 %while.5 = (s32[]{:T(128)}, bf16[1024,128]{1,0:T(8,128)(2,1)S(1)}, s32[5,2]{0,1:T(2,128)S(1)}, bf16[5,512,128]{2,1,0:T(8,128)(2,1)S(1)}, s32[]{:T(128)}) while((s32[]{:T(128)}, bf16[1024,128]{1,0:T(8,128)(2,1)S(1)}, s32[5,2]{0,1:T(2,128)S(1)}, bf16[5,512,128]{2,1,0:T(8,128)(2,1)S(1)}, s32[]{:T(128)}) %tuple.112), condition=%wide.while_cond.1, body=%wide.while_body.1.sunk | while | flops 2 | bytes 262249 | solution.py:43
  141.9 0.7 bitcast_dynamic-update-slice_fusion.9
  143.3 0.7 bitcast_dynamic-update-slice_fusion.9
  144.7 0.7 bitcast_dynamic-update-slice_fusion.9
  146.2 0.7 bitcast_dynamic-update-slice_fusion.9
  147.6 0.7 bitcast_dynamic-update-slice_fusion.9
  148.4 1.0 copy.84
  149.4 2.6 fusion.33
  152.0 2.6 fusion.35
  154.7 0.7 all-gather.3.cloned.1.call-done
  155.3 2.8 fusion.29
  158.2 5.0 %fusion.32 = (f32[512]{0:T(512)S(1)}, f32[512,4096]{1,0:T(8,128)}) fusion(pred[512,4096]{1,0:T(32,128)(4,1)S(1)} %copy-done.1, bf16[4096,128]{1,0:T(8,128)(2,1)S(1)} %bitcast.135, bf16[512,2,128]{2,0,1:T(8,128)(2,1)S(1)} %bitcast.141), kind=kOutput, calls=%fused_computation.87 | convolution fusion | flops 543161856 | bytes 11667456 | tf_op jit(solution)/shard_map/dot_general | solution.py:35
  163.3 5.5 %fusion.2 = (f32[512]{0:T(512)S(1)}, bf16[512,4096]{1,0:T(8,128)(2,1)}) fusion(f32[512,4096]{1,0:T(8,128)} %get-tuple-element.180, f32[512]{0:T(512)S(1)} %max.22), kind=kLoop, calls=%fused_computation.14 | loop fusion | flops 6290944 | bytes 12587008 | tf_op jit(solution)/shard_map/reduce_sum | solution.py:67
  168.8 1.5 fusion.12
  170.4 1.9 convolution_bitcast_fusion
  172.2 67.1 %all-gather.5.cloned.1.call-done = bf16[2,64,64,128]{3,2,1,0:T(8,128)(2,1)} async-done(((bf16[2,1,64,128]{3,2,1,0:T(8,128)(2,1)}), bf16[2,64,64,128]{3,2,1,0:T(8,128)(2,1)}) %all-gather.5.cloned.1.call-update) | async-done | bytes 2097168 | tf_op jit(solution)/shard_map/all_gather | solution.py:134
  239.3 2.9 fusion.28
  242.2 1.3 fusion.15
  243.7 5.0 %fusion.34 = (f32[512]{0:T(512)S(1)}, f32[512,4096]{1,0:T(8,128)}) fusion(pred[512,4096]{1,0:T(32,128)(4,1)S(1)} %broadcast_in_dim.28, bf16[4096,128]{1,0:T(8,128)(2,1)S(1)} %bitcast.134, bf16[512,2,128]{2,0,1:T(8,128)(2,1)S(1)} %bitcast.142), kind=kOutput, calls=%fused_computation.89 | convolution fusion | flops 543161856 | bytes 11667456 | tf_op jit(solution)/shard_map/dot_general | solution.py:35
  248.8 1.5 fusion.10
  250.3 1.7 convolution_bitcast_fusion.1
  252.0 5.5 %fusion = (f32[512]{0:T(512)S(1)}, bf16[512,4096]{1,0:T(8,128)(2,1)}) fusion(f32[512,4096]{1,0:T(8,128)} %get-tuple-element.184, f32[512]{0:T(512)S(1)} %max.20), kind=kLoop, calls=%fused_computation.12 | loop fusion | flops 6290944 | bytes 12587008 | tf_op jit(solution)/shard_map/reduce_sum | solution.py:67
  257.6 3.4 %fusion.14 = bf16[8,64,128]{2,1,0:T(8,128)(2,1)S(1)} fusion(f32[8,64,128]{2,1,0:T(8,128)S(1)} %convolution_bitcast_fusion.1, bf16[8,64,4096]{2,1,0:T(8,128)(2,1)} %bitcast.137, bf16[4096,128,1]{1,0,2:T(8,128)(2,1)S(1)} %bitcast.148, f32[8,64]{1,0:T(8,128)S(1)} %add.90), kind=kOutput, calls=%fused_computation.34 | convolution fusion | flops 537067520 | bytes 5638144 | tf_op jit(solution)/shard_map/dot_general | solution.py:70
  261.9 18.1 %all_to_all.33 = bf16[512,2,128]{2,1,0:T(2,128)(2,1)S(1)} all-to-all(bf16[512,2,128]{2,1,0:T(2,128)(2,1)S(1)} %pad_maximum_fusion.2), channel_id=1, replica_groups=mesh['seq'=64,'head'=8] {'head'}, dimensions={0} | all-to-all | bytes 524288 | tf_op jit(solution)/shard_map/all_to_all | solution.py:158
  280.2 0.9 reshape.390
  (109 shorter events, 17.6 us)
Async XLA Ops:
  6.5 68.3 %copy-start = (bf16[64,2048]{1,0:T(8,128)(2,1)S(1)}, bf16[64,2048]{1,0:T(8,128)(2,1)}, u32[]{:S(2)}) copy-start(bf16[64,2048]{1,0:T(8,128)(2,1)} %param.5) | copy-start | bytes 786436
  6.5 148.8 %all-gather.3.cloned.1.call-start = ((), (), s32[]{:S(2)}) async-start(), calls=%async_computation.2 | async-start | bytes 2129920 | tf_op jit(solution)/shard_map/all_gather | solution.py:133
  32.7 49.7 %copy-start.8 = (s32[16,5]{0,1:T(8,128)S(1)}, s32[16,5]{0,1:T(8,128)}, u32[]{:S(2)}) copy-start(s32[16,5]{0,1:T(8,128)} %param.9) | copy-start | bytes 964
  56.7 57.8 %collective-permute-start = (bf16[512,1,128]{0,2,1:T(8,128)(2,1)S(1)}, bf16[512,1,128]{0,2,1:T(8,128)(2,1)S(1)}, u32[]{:S(2)}, u32[]{:S(2)}) collective-permute-start(bf16[512,1,128]{0,2,1:T(8,128)(2,1)S(1)} %constant_dynamic-slice_fusion.5), channel_id=1, source_target_pairs={{0,8},{8,16},{16,24},{24,32},{32,40},{40,48},{48,56},{56,64},{64,7... | collective-permute-start | bytes 393224 | tf_op jit(solution)/shard_map/ppermute | solution.py:16
  72.9 47.8 %collective-permute-start.1 = (bf16[512,1,128]{0,2,1:T(8,128)(2,1)}, bf16[512,1,128]{0,2,1:T(8,128)(2,1)}, u32[]{:S(2)}, u32[]{:S(2)}) collective-permute-start(bf16[512,1,128]{0,2,1:T(8,128)(2,1)} %constant_dynamic-slice_fusion.4), channel_id=1, source_target_pairs={{0,8},{8,16},{16,24},{24,32},{32,40},{40,48},{48,56},{56,64},{64,7... | collective-permute-start | bytes 393224 | tf_op jit(solution)/shard_map/ppermute | solution.py:16
  75.6 72.7 %all-to-all-start = ((bf16[64,16,128]{2,0,1:T(8,128)(2,1)}), bf16[64,16,128]{2,0,1:T(8,128)(2,1)}, u32[]{:S(2)}, u32[]{:S(2)}) async-start(bf16[64,16,128]{2,0,1:T(8,128)(2,1)} %copy_bitcast_fusion), calls=%async_computation | async-start | bytes 524288 | tf_op jit(solution)/shard_map/all_to_all | solution.py:88
  80.9 158.5 %all-gather.5.cloned.1.call-start = ((), (), s32[]{:S(2)}) async-start(), calls=%async_computation.3 | async-start | bytes 2129920 | tf_op jit(solution)/shard_map/all_gather | solution.py:134
  114.7 6.8 %copy-start.7 = (bf16[512,128]{0,1:T(8,128)(2,1)S(1)}, bf16[512,128]{0,1:T(8,128)(2,1)}, u32[]{:S(2)}) copy-start(bf16[512,128]{0,1:T(8,128)(2,1)} %fusion.44) | copy-start | bytes 393220
  120.7 0.9 copy-start.6
  129.9 1.0 copy-start.4
  130.9 18.5 %copy-start.9 = (pred[8,5]{1,0:T(8,128)(4,1)S(1)}, pred[8,5]{1,0:T(8,128)(4,1)}, u32[]{:S(2)}) copy-start(pred[8,5]{1,0:T(8,128)(4,1)} %get-tuple-element.178) | copy-start | bytes 124
  155.3 2.8 copy-start.1
  239.3 2.9 copy-start.3
  242.2 1.5 copy-start.2
  252.0 5.6 %copy-start.5 = (bf16[1,64,64,128]{3,2,1,0:T(8,128)(2,1)S(1)}, bf16[1,64,64,128]{3,2,1,0:T(8,128)(2,1)}, u32[]{:S(2)}) copy-start(bf16[1,64,64,128]{3,2,1,0:T(8,128)(2,1)} %get-tuple-element.157) | copy-start | bytes 3145732
Sparse Core Ops, SparseCore 0:
  56.8 98.4 all-gather.2
  158.7 80.5 all-gather.4
where the time goes:
time: 289 us; the launch traced here: 288 us
  local copies, waits for them, and re-layouts  75.8 us (26%)
  waiting for transfers between devices  67.9 us (23%)
  blocking collectives  60 us (21%)
  starting transfers between devices  23.4 us (8%)
  matrix products  23.4 us (8%)
  other arithmetic  19.5 us (7%)
  between operations  17.7 us (6%)
    all_gather x1, waiting for transfers between devices, body(): lax.all_gather(picked_values, 'seq', axis=1, tiled=True)  67.1 us
    gather x60, local copies, waits for them, and re-layouts  30.1 us
    broadcast_in_dim x4, local copies, waits for them, and re-layouts, attend_head(): vert_scores = jnp.where(vert_keep[:, None, :, None], vert_scores, -jnp.inf)  29.5 us
    all_gather x1, blocking collectives, body(): lax.all_gather(keys, 'head', axis=0, tiled=True)  21.9 us
    all_gather x1, blocking collectives, body(): lax.all_gather(values, 'head', axis=0, tiled=True)  20 us
    ppermute x2, starting transfers between devices, passed_along(): return lax.ppermute(block, axis, route)  18.2 us
    all_to_all x1, blocking collectives, body(): lax.all_to_all(piled_matrix, 'head', split_axis=0, concat_axis=1, tiled=T...  18.1 us
    reduce_sum x2, other arithmetic, attend_head(): jnp.sum(vert_weights, axis=(2, 3)) + jnp.sum(slash_weights, axis=(2, 3))  11 us
  transfers between devices with their start and end apart: 5, of which 2 were waited for; matrix products, arithmetic and copies ran while one was open for 31% of the time, Pallas kernels for 0%

commit v1 on v0

v1 whole, which is shorter than its diff:
```python
import functools
import math

import jax
import jax.numpy as jnp
from jax import lax
from jax.experimental import pallas as pl
from jax.experimental.pallas import tpu as pltpu
from jax.sharding import PartitionSpec as P

HDIM = 128
BLOCK = 64
NX, NZ, NC = 4, 8, 2
LOW = -1e30
RATE = HDIM ** (-0.5) * math.log2(math.e)
MESH = pl.DeviceIdType.MESH


def kernel(
    ny,
    ns,
    q_ref,
    k_ref,
    v_ref,
    vert_ref,
    offs_ref,
    out_ref,
    qbuf,
    own_k,
    own_v,
    raw,
    prior,
    vert,
    bias_l,
    score_l,
    score_a,
    score_b,
    peak,
    sums,
    acc,
    obuf,
    y_send,
    y_recv,
    ring_send,
    ring_recv,
    bx_send,
    bx_recv,
    az_send,
    az_recv,
    sib_send,
    sib_recv,
    misc,
    out_send,
    out_recv,
):
    s = lax.axis_index("seq")
    j = lax.axis_index("head")
    core = lax.rem(s, NC)
    z = lax.rem(s // NC, NZ)
    x = s // (NC * NZ)
    nseq = NX * NZ * NC
    rows = ny * BLOCK
    own = (own_k, own_v)

    def at(px, pz, pc):
        return (lax.rem(px + NX, NX) * NZ + lax.rem(pz + NZ, NZ)) * NC + pc

    up_z, dn_z = at(x, z + 1, core), at(x, z - 1, core)
    up_x, dn_x = at(x + 1, z, core), at(x - 1, z, core)
    sib = at(x, z, 1 - core)
    after = lax.rem(s + 1, nseq)
    before = lax.rem(s + nseq - 1, nseq)
    across_x = [at(x + r, z, core) for r in range(1, NX)]
    reach = NZ // 2 - 1
    along_z = {d: at(x, z + d, core) for r in range(1, reach + 1) for d in (r, -r)}
    far_z = {d: other for d, other in along_z.items() if abs(d) > 1}

    kv_col = pl.multiple_of((j // 2) * HDIM, HDIM)
    q_col = pl.multiple_of(j * 2 * HDIM, 2 * HDIM)
    here = [
        pltpu.make_async_copy(k_ref.at[:, pl.ds(kv_col, HDIM)], own_k.at[j], misc.at[0]),
        pltpu.make_async_copy(v_ref.at[:, pl.ds(kv_col, HDIM)], own_v.at[j], misc.at[1]),
        pltpu.make_async_copy(q_ref.at[:, pl.ds(q_col, 2 * HDIM)], qbuf.at[j], misc.at[2]),
    ]
    for copy in here:
        copy.start()

    barrier = pltpu.get_barrier_semaphore()
    for r in range(1, ny):
        pl.semaphore_signal(
            barrier, inc=1, device_id=(s, lax.rem(j + r, ny)), device_id_type=MESH
        )
    others = [up_z, dn_z, sib, after, before] + across_x + list(far_z.values())
    for other in others:
        pl.semaphore_signal(barrier, inc=1, device_id=(other, j), device_id_type=MESH)
    pl.semaphore_wait(barrier, ny - 1 + len(others))

    sent = []

    def remote(src, dst, device, send_sem, recv_sem):
        copy = pltpu.make_async_remote_copy(
            src, dst, send_sem, recv_sem, device_id=device, device_id_type=MESH
        )
        copy.start()
        sent.append(copy)

    def send(src, to, send_sem, recv_sem):
        remote(src, src, (to, j), send_sem, recv_sem)

    def arrived(dst, sem):
        pltpu.make_async_copy(dst, dst, sem).wait()

    order = sorted(range(1, ny), key=lambda r: -min(r, ny - r))

    def y_start(kind):
        for r in order:
            to = lax.rem(j + r, ny)
            if kind == 3:
                col = pl.multiple_of((to // 2) * HDIM, HDIM)
                src, dst = raw.at[:, :, pl.ds(col, HDIM)], prior.at[:, j]
            elif kind == 2:
                col = pl.multiple_of(to * 2 * HDIM, 2 * HDIM)
                src, dst = q_ref.at[:, pl.ds(col, 2 * HDIM)], qbuf.at[j]
            else:
                col = pl.multiple_of((to // 2) * HDIM, HDIM)
                src, dst = (k_ref, v_ref)[kind].at[:, pl.ds(col, HDIM)], own[kind].at[j]
            remote(src, dst, (s, to), y_send.at[kind, to], y_recv.at[kind, j])

    def y_wait(kind):
        here[kind].wait()
        for r in order:
            source = lax.rem(j + ny - r, ny)
            if kind == 3:
                dst = prior.at[:, source]
            else:
                dst = qbuf.at[source] if kind == 2 else own[kind].at[source]
            arrived(dst, y_recv.at[kind, source])

    class Ring:
        def __init__(self, kind, index, slot, n, pos, up, dn, halves, last=1):
            self.sems = (ring_send.at[kind, index], ring_recv.at[kind, index])
            self.slot, self.n, self.pos = slot, n, pos
            self.up, self.dn, self.half, self.halves = up, dn, n // 2, halves
            self.last = last

        def part(self, which, direction, t):
            ref = self.slot(lax.rem(which + self.n, self.n))
            if t < self.half:
                return ref
            if self.halves is not None:
                return ref.at[pl.ds(direction * self.halves, self.halves)]
            return ref if direction == self.last else None

        def start(self, t):
            for direction, sign, to in ((0, -1, self.up), (1, 1, self.dn)):
                part = self.part(self.pos + sign * (t - 1), direction, t)
                if part is not None:
                    sems = [sem.at[direction, t - 1] for sem in self.sems]
                    send(part, to, *sems)

        def wait(self, t):
            for direction, sign in ((0, -1), (1, 1)):
                part = self.part(self.pos + sign * t, direction, t)
                if part is not None:
                    arrived(part, self.sems[1].at[direction, t - 1])

    class Gather:
        def __init__(self, kind):
            self.kind = kind
            self.ax = Ring(
                kind, 0, lambda i: vert.at[kind, 0, core, i], NX, x, up_x, dn_x, NZ // 2
            )
            self.bz = Ring(
                kind, 1, lambda i: vert.at[kind, 1, core, :, i], NZ, z, up_z, dn_z, None, kind
            )
            self.pending = {}

        def row(self, pc, shift):
            return vert.at[self.kind, 0, pc, lax.rem(x + shift + NX, NX)]

        def bundle(self, pc, shift):
            return vert.at[self.kind, 1, pc, :, lax.rem(z + shift + NZ, NZ)]

        def share(self, line, shift):
            n = len(self.pending)
            chunk = self.row if line == 0 else self.bundle
            send(chunk(core, shift), sib, sib_send.at[self.kind, n], sib_recv.at[self.kind, n])
            self.pending[(line, shift)] = n

        def shared(self, line, shift):
            chunk = self.row if line == 0 else self.bundle
            arrived(chunk(1 - core, shift), sib_recv.at[self.kind, self.pending[(line, shift)]])

        def pick(self):
            for m in range(2):
                which = jnp.clip(vert_ref[2 * j + m, s] - s * ny, 0, ny - 1)
                vert[self.kind, m, core, x, z] = own[self.kind][which]

        def line_a(self, n):
            block = lambda i: vert.at[self.kind, 0, core, x, lax.rem(i + NZ, NZ)]
            sems = (az_send.at[self.kind], az_recv.at[self.kind])
            last_x = NX // 2
            sign = 1 if self.kind == 0 else -1
            if n == 0:
                for r in range(reach, 0, -1):
                    for d in (r, -r):
                        send(block(z), along_z[d], sems[0].at[reach + d], sems[1].at[reach + d])
            elif n == 1:
                for r in range(1, reach + 1):
                    for d in (r, -r):
                        arrived(block(z - d), sems[1].at[reach + d])
                to = up_z if sign == 1 else dn_z
                send(block(z - sign * reach), to, sems[0].at[reach], sems[1].at[reach])
            elif n == 2:
                arrived(block(z - sign * (reach + 1)), sems[1].at[reach])
                self.ax.start(1)
                self.share(0, 0)
            else:
                t = n - 2
                if t > last_x:
                    return
                self.ax.wait(t)
                if t < last_x:
                    self.ax.start(t + 1)
                    self.share(0, -t)
                self.share(0, t)

        def line_b(self, n):
            own_chunk = lambda i: vert.at[self.kind, 1, core, lax.rem(i + NX, NX), z]
            sems = (bx_send.at[self.kind], bx_recv.at[self.kind])
            if n == 0:
                for r in range(1, NX):
                    send(own_chunk(x), across_x[r - 1], sems[0].at[r - 1], sems[1].at[r - 1])
            elif n == 1:
                for r in range(1, NX):
                    arrived(own_chunk(x - r), sems[1].at[r - 1])
                self.bz.start(1)
                self.share(1, 0)
            else:
                t = n - 1
                if t > NZ // 2:
                    return
                self.bz.wait(t)
                if t < NZ // 2:
                    self.bz.start(t + 1)
                    self.share(1, -t)
                self.share(1, t)

        def step(self, n):
            self.line_b(n)
            self.line_a(n)

    nt = (((1,), (1,)), ((), ()))
    chunk = ny * BLOCK

    def group(i):
        return slice(i * HDIM, (i + 1) * HDIM)

    def lanes(value, op):
        return functools.reduce(op, [value[:, group(i)] for i in range(value.shape[1] // HDIM)])

    def queries_of(m):
        return qbuf[:, :, m * HDIM : (m + 1) * HDIM].reshape(rows, HDIM)

    def set_near():
        shape = (ny, 2 * chunk)
        place = lax.broadcasted_iota(jnp.int32, shape, 1) // BLOCK
        dist = ny + lax.broadcasted_iota(jnp.int32, shape, 0) - place
        seg_then = jnp.maximum(s - 1, 0)
        least = jnp.where(s > 0, 0, ny)
        for m in range(2):
            head = 2 * j + m
            then = vert_ref[head, seg_then] - seg_then * ny
            now = vert_ref[head, s] - s * ny + ny
            keep = (dist > 0) & ((place == then) | (place == now))
            for i in range(ns):
                keep = keep | (dist == offs_ref[i, head])
            bias_l[m] = jnp.where(keep & (place >= least), 0.0, LOW)

    def near_scores(m, half):
        keys = (prior[0] if half == 0 else own_k[...]).reshape(chunk, HDIM)
        value = lax.dot_general(queries_of(m), keys, nt, preferred_element_type=jnp.float32)
        bias = bias_l[m, :, half * chunk : (half + 1) * chunk]
        value = (value.reshape(ny, BLOCK, chunk) + bias[:, None, :]).reshape(rows, chunk)
        if half == 1:
            line = lax.broadcasted_iota(jnp.int32, (rows, chunk), 0)
            value = jnp.where(
                lax.broadcasted_iota(jnp.int32, (rows, chunk), 1) <= line, value, LOW
            )
        score_l[m, half] = value
        peak[m] = jnp.maximum(peak[m], lanes(value, jnp.maximum))

    def near_values(m, half):
        values = (prior[1] if half == 0 else own_v[...]).reshape(chunk, HDIM)
        top = peak[m]
        parts = [
            jnp.exp2(score_l[m, half, :, group(g)] * RATE - top) for g in range(chunk // HDIM)
        ]
        weight = jnp.concatenate([part.astype(jnp.bfloat16) for part in parts], axis=1)
        sums[m] += functools.reduce(jnp.add, parts)
        acc[m] += jnp.dot(weight, values, preferred_element_type=jnp.float32)

    def far_chunk(m, shift, pc):
        before_here = jnp.maximum((s - pc + NC) // NC - 1, 0)
        if m == 0:
            px = lax.rem(x + shift + NX, NX)
            piece = lax.broadcasted_iota(jnp.int32, (1, NZ * BLOCK), 1) // BLOCK
            return (pc, px), pc * NX + px, px * NZ + piece < before_here, NZ * BLOCK
        pz = lax.rem(z + shift + NZ, NZ)
        piece = lax.broadcasted_iota(jnp.int32, (1, NX * BLOCK), 1) // BLOCK
        where = (pc, slice(None), pz)
        return where, pc * NZ + pz, piece * NZ + pz < before_here, NX * BLOCK

    def far_scores(m, shift):
        store = (score_a, score_b)[m]

        def step(pc, carry):
            where, slot, keep, size = far_chunk(m, shift, pc)
            keys = vert[(0, m) + where].reshape(size, HDIM)
            value = lax.dot_general(queries_of(m), keys, nt, preferred_element_type=jnp.float32)
            value = value + jnp.where(keep, 0.0, LOW)
            store[slot] = value
            peak[m] = jnp.maximum(peak[m], lanes(value, jnp.maximum))
            return carry

        lax.fori_loop(0, NC, step, 0)

    def far_values(m, pc):
        store = (score_a, score_b)[m]

        def step(shift, carry):
            where, slot, _, size = far_chunk(m, shift, pc)
            values = vert[(1, m) + where].reshape(size, HDIM)
            top = peak[m]
            parts = [
                jnp.exp2(store[slot, :, group(g)] * RATE - top) for g in range(size // HDIM)
            ]
            weight = jnp.concatenate([part.astype(jnp.bfloat16) for part in parts], axis=1)
            sums[m] += functools.reduce(jnp.add, parts)
            acc[m] += jnp.dot(weight, values, preferred_element_type=jnp.float32)
            return carry

        lax.fori_loop(0, (NX, NZ)[m], step, 0)

    def set_top(m):
        top = jnp.max(peak[m], axis=1, keepdims=True) * RATE
        peak[m] = jnp.broadcast_to(top, (rows, HDIM))

    stays = []

    def finish(m):
        total = jnp.sum(sums[m], axis=1, keepdims=True)
        obuf[m] = (acc[m] / total).astype(jnp.bfloat16).reshape(ny, BLOCK, HDIM)
        my_col = pl.ds(pl.multiple_of((2 * j + m) * HDIM, HDIM), HDIM)
        for r in order:
            to = lax.rem(j + r, ny)
            remote(
                obuf.at[m, to],
                out_ref.at[:, my_col],
                (s, to),
                out_send.at[m, to],
                out_recv.at[m, j],
            )
        stay = pltpu.make_async_copy(obuf.at[m, j], out_ref.at[:, my_col], misc.at[7 + m])
        stay.start()
        stays.append(stay)

    keys, values = Gather(0), Gather(1)

    def far_shifts(t, n):
        return [0] if t == 0 else [t] if t == n // 2 else [-t, t]

    def scores_of(m, t):
        for shift in far_shifts(t, (NX, NZ)[m]):
            keys.shared(m, shift)
            far_scores(m, shift)

    def values_of(m):
        far_values(m, core)
        for t in range((NX, NZ)[m] // 2 + 1):
            for shift in far_shifts(t, (NX, NZ)[m]):
                values.shared(m, shift)
        far_values(m, 1 - core)

    for kind in range(2):
        remote((k_ref, v_ref)[kind], raw.at[kind], (after, j), misc.at[3 + kind], misc.at[5 + kind])
        y_start(kind)
    peak[...] = jnp.full(peak.shape, LOW, jnp.float32)
    sums[...] = jnp.zeros(sums.shape, jnp.float32)
    acc[...] = jnp.zeros(acc.shape, jnp.float32)
    y_wait(0)
    keys.pick()
    keys.step(0)
    y_wait(1)
    values.pick()
    values.step(0)
    y_start(2)
    for kind in range(2):
        arrived(raw.at[kind], misc.at[5 + kind])
    y_start(3)
    here.append(
        pltpu.make_async_copy(raw.at[:, :, pl.ds(kv_col, HDIM)], prior.at[:, j], misc.at[9])
    )
    here[3].start()
    set_near()

    half_x, half_z = NX // 2, NZ // 2
    steps = max(half_z + 1, half_x + 2)
    work = [
        (3, lambda: y_wait(2)),
        (3, lambda: near_scores(1, 1)),
        (3, lambda: scores_of(1, 0)),
        (3, lambda: near_scores(0, 1)),
    ]
    for t in range(1, half_z + 1):
        work.append((max(4, t + 2), lambda t=t: scores_of(1, t)))
    for t in range(half_x + 1):
        work.append((t + 4, lambda t=t: scores_of(0, t)))
    work.append((steps, lambda: (y_wait(3), near_scores(1, 0), near_scores(0, 0))))
    for n in range(1, steps + 1):
        keys.step(n)
        if n > 1:
            values.step(n - 1)
        for due, unit in work:
            if due == n or (n == steps and due > n):
                unit()
    values.step(steps)
    for m in (1, 0):
        set_top(m)
        near_values(m, 1)
        near_values(m, 0)
        values_of(m)
        finish(m)

    for m in (1, 0):
        for r in order:
            source = lax.rem(j + ny - r, ny)
            col = pl.ds(pl.multiple_of((2 * source + m) * HDIM, HDIM), HDIM)
            arrived(out_ref.at[:, col], out_recv.at[m, source])
    for copy in stays:
        copy.wait()
    for copy in sent:
        copy.wait_send()


def body(queries, keys, values, vertical, offsets):
    ny = lax.axis_size("head")
    ns = offsets.shape[1]
    rows = ny * BLOCK
    nsib = NX + NZ
    half = max(NX, NZ) // 2
    bf16, f32, dma = jnp.bfloat16, jnp.float32, pltpu.SemaphoreType.DMA
    hbm = pl.BlockSpec(memory_space=pltpu.HBM)
    small = pl.BlockSpec(memory_space=pltpu.SMEM)
    segment = pltpu.VMEM((ny, BLOCK, HDIM), bf16)
    return pl.pallas_call(
        functools.partial(kernel, ny, ns),
        out_shape=jax.ShapeDtypeStruct(queries.shape, bf16),
        in_specs=[hbm, hbm, hbm, small, small],
        out_specs=pl.BlockSpec(memory_space=pl.ANY),
        scratch_shapes=[
            pltpu.VMEM((ny, BLOCK, 2 * HDIM), bf16),
            segment,
            segment,
            pltpu.VMEM((2,) + keys.shape, bf16),
            pltpu.VMEM((2, ny, BLOCK, HDIM), bf16),
            pltpu.VMEM((2, 2, NC, NX, NZ, BLOCK, HDIM), bf16),
            pltpu.VMEM((2, ny, 2 * rows), f32),
            pltpu.VMEM((2, 2, rows, rows), f32),
            pltpu.VMEM((NC * NX, rows, NZ * BLOCK), f32),
            pltpu.VMEM((NC * NZ, rows, NX * BLOCK), f32),
            pltpu.VMEM((2, rows, HDIM), f32),
            pltpu.VMEM((2, rows, HDIM), f32),
            pltpu.VMEM((2, rows, HDIM), f32),
            pltpu.VMEM((2, ny, BLOCK, HDIM), bf16),
            dma((4, ny)),
            dma((4, ny)),
            dma((2, 2, 2, half)),
            dma((2, 2, 2, half)),
            dma((2, NX - 1)),
            dma((2, NX - 1)),
            dma((2, NZ - 1)),
            dma((2, NZ - 1)),
            dma((2, nsib)),
            dma((2, nsib)),
            dma((10,)),
            dma((2, ny)),
            dma((2, ny)),
        ],
        compiler_params=pltpu.CompilerParams(
            collective_id=0, has_side_effects=True, vmem_limit_bytes=58 * 1024 * 1024
        ),
    )(queries, keys, values, vertical, offsets.T)


def solution(mesh):
    whole = P(("seq", "head"), None)
    return jax.shard_map(
        body,
        mesh=mesh,
        in_specs=(whole, whole, whole, P(), P()),
        out_specs=whole,
        check_vma=False,
    )
```

time: 289 us -> 66 us (0.23)
  local copies, waits for them, and re-layouts: 75.8 us -> 1.67 us
  waiting for transfers between devices: 67.9 us -> 0 us
  Pallas kernels: 0 us -> 64.1 us
  blocking collectives: 60 us -> 0 us
  matrix products: 23.4 us -> 0 us
  starting transfers between devices: 23.4 us -> 0 us
  other arithmetic: 19.5 us -> 0 us
  between operations: 17.7 us -> 0.01 us
    all_gather x2 -> x0, waiting for transfers between devices: 67.8 us -> none  [the longest x1 67.1 us: body(): lax.all_gather(picked_values, 'seq', axis=1, tiled=True)]
    pallas_call x0 -> x1, Pallas kernels: none -> 64.1 us  [body(): pl.pallas_call(functools.partial(kernel, ny, ns), out_shape=jax.ShapeDtyp...]
    all_gather x2 -> x0, blocking collectives: 41.9 us -> none  [the longest x1 21.9 us: body(): lax.all_gather(keys, 'head', axis=0, tiled=True)]
    gather x60 -> x0, local copies, waits for them, and re-layouts: 30.1 us -> none
    broadcast_in_dim x4 -> x0, local copies, waits for them, and re-layouts: 29.5 us -> none  [attend_head(): vert_scores = jnp.where(vert_keep[:, None, :, None], vert_scores, -jnp.inf)]
    dot_general x8 -> x0, matrix products: 23.4 us -> none  [the longest x2 10 us: attend_head(): jnp.dot(head_queries, flat_keys.T, preferred_element_type=jnp.float32)]
    ppermute x2 -> x0, starting transfers between devices: 18.2 us -> none  [passed_along(): return lax.ppermute(block, axis, route)]
    all_to_all x1 -> x0, blocking collectives: 18.1 us -> none  [body(): lax.all_to_all(piled_matrix, 'head', split_axis=0, concat_axis=1, tiled=T...]
  transfers between devices with their start and end apart: 5 -> 0, of which waited for: 2 -> 0; matrix products, arithmetic and copies ran while one was open for 31% -> 0% of each run, Pallas kernels for 0% -> 0%
where the time goes in v1:
time: 66 us; the launch traced here: 65.8 us
  Pallas kernels  64.1 us (97%)
  local copies, waits for them, and re-layouts  1.67 us (3%)
    pallas_call x1, Pallas kernels, body(): pl.pallas_call(functools.partial(kernel, ny, ns), out_shape=jax.ShapeDtyp...  64.1 us
    unnamed x1, local copies, waits for them, and re-layouts  1.67 us

profile of v1, /device:TPU:1, one launch (start us, length us, event | category | flops | bytes accessed | tf_op | source)
XLA Modules:
  0.0 65.8 jit_solution(3265558066870747598)
XLA Ops:
  0.0 64.1 %shard_map.55 = bf16[64,2048]{1,0:T(8,128)(2,1)} custom-call(bf16[64,2048]{1,0:T(8,128)(2,1)} %q_ref.1, bf16[64,512]{1,0:T(8,128)(2,1)} %k_ref.1, bf16[64,512]{1,0:T(8,128)(2,1)} %v_ref.1, s32[16,64]{1,0:T(8,128)} %vert_ref.1, s32[5,16]{1,0:T(8,128)} %bitcast.1), custom_call_target="tpu_custom_call" | custom-call | tf_op jit(solution)/shard_map/pallas_call | solution.py:456
  64.1 1.7 %copy.7 = bf16[64,2048]{1,0:T(8,128)(2,1)} copy(bf16[64,2048]{1,0:T(8,128)(2,1)} %shard_map.55) | data formatting | bytes 524288

commit v2 on v1

--- a/solution.py
+++ b/solution.py
@@ -71,7 +71,7 @@
     after = lax.rem(s + 1, nseq)
     before = lax.rem(s + nseq - 1, nseq)
     across_x = [at(x + r, z, core) for r in range(1, NX)]
-    reach = NZ // 2 - 1
+    reach = NZ // 4
     along_z = {d: at(x, z + d, core) for r in range(1, reach + 1) for d in (r, -r)}
     far_z = {d: other for d, other in along_z.items() if abs(d) > 1}
 
@@ -115,10 +115,7 @@
     def y_start(kind):
         for r in order:
             to = lax.rem(j + r, ny)
-            if kind == 3:
-                col = pl.multiple_of((to // 2) * HDIM, HDIM)
-                src, dst = raw.at[:, :, pl.ds(col, HDIM)], prior.at[:, j]
-            elif kind == 2:
+            if kind == 2:
                 col = pl.multiple_of(to * 2 * HDIM, 2 * HDIM)
                 src, dst = q_ref.at[:, pl.ds(col, 2 * HDIM)], qbuf.at[j]
             else:
@@ -130,11 +127,85 @@
         here[kind].wait()
         for r in order:
             source = lax.rem(j + ny - r, ny)
-            if kind == 3:
-                dst = prior.at[:, source]
-            else:
-                dst = qbuf.at[source] if kind == 2 else own[kind].at[source]
+            dst = qbuf.at[source] if kind == 2 else own[kind].at[source]
             arrived(dst, y_recv.at[kind, source])
+
+    def to_next(kind):
+        return pltpu.make_async_remote_copy(
+            (k_ref, v_ref)[kind],
+            raw.at[kind],
+            misc.at[3 + kind],
+            misc.at[5 + kind],
+            device_id=(after, j),
+            device_id_type=MESH,
+        )
+
+    def to_sibling(kind):
+        return pltpu.make_async_remote_copy(
+            own[kind],
+            prior.at[kind],
+            misc.at[3 + kind],
+            misc.at[5 + kind],
+            device_id=(after, j),
+            device_id_type=MESH,
+        )
+
+    def spread(r):
+        to = lax.rem(j + r, ny)
+        col = pl.multiple_of((to // 2) * HDIM, HDIM)
+        return pltpu.make_async_remote_copy(
+            raw.at[:, :, pl.ds(col, HDIM)],
+            prior.at[:, j],
+            y_send.at[3, to],
+            y_recv.at[3, j],
+            device_id=(s, to),
+            device_id_type=MESH,
+        )
+
+    spread_own = pltpu.make_async_copy(
+        raw.at[:, :, pl.ds(kv_col, HDIM)], prior.at[:, j], misc.at[9]
+    )
+
+    def start_prior(kind, early):
+        if early:
+            pl.when(core == NC - 1)(lambda: to_next(kind).start())
+        else:
+            pl.when(core == 0)(lambda: to_sibling(kind).start())
+
+    def spread_prior():
+        @pl.when(core == 0)
+        def _():
+            for kind in range(2):
+                arrived(raw.at[kind], misc.at[5 + kind])
+            for r in order:
+                spread(r).start()
+            spread_own.start()
+
+    def take_prior():
+        @pl.when(core == 0)
+        def _():
+            for r in order:
+                source = lax.rem(j + ny - r, ny)
+                arrived(prior.at[:, source], y_recv.at[3, source])
+            spread_own.wait()
+
+        @pl.when(core == NC - 1)
+        def _():
+            for kind in range(2):
+                arrived(prior.at[kind], misc.at[5 + kind])
+
+    def end_prior():
+        @pl.when(core == 0)
+        def _():
+            for kind in range(2):
+                to_sibling(kind).wait_send()
+            for r in order:
+                spread(r).wait_send()
+
+        @pl.when(core == NC - 1)
+        def _():
+            for kind in range(2):
+                to_next(kind).wait_send()
 
     class Ring:
         def __init__(self, kind, index, slot, n, pos, up, dn, halves, last=1):
@@ -200,19 +271,32 @@
             block = lambda i: vert.at[self.kind, 0, core, x, lax.rem(i + NZ, NZ)]
             sems = (az_send.at[self.kind], az_recv.at[self.kind])
             last_x = NX // 2
-            sign = 1 if self.kind == 0 else -1
+            side = 1 if self.kind == 0 else -1
+            handed = [
+                (sign, r)
+                for r in range(reach, 0, -1)
+                for sign in (1, -1)
+                if reach + r < NZ // 2 or sign == side
+            ]
             if n == 0:
                 for r in range(reach, 0, -1):
                     for d in (r, -r):
-                        send(block(z), along_z[d], sems[0].at[reach + d], sems[1].at[reach + d])
+                        spot = NZ // 2 + d
+                        send(block(z), along_z[d], sems[0].at[spot], sems[1].at[spot])
             elif n == 1:
-                for r in range(1, reach + 1):
+                for r in range(reach, 0, -1):
                     for d in (r, -r):
-                        arrived(block(z - d), sems[1].at[reach + d])
-                to = up_z if sign == 1 else dn_z
-                send(block(z - sign * reach), to, sems[0].at[reach], sems[1].at[reach])
+                        arrived(block(z - d), sems[1].at[NZ // 2 + d])
+                    if r == reach:
+                        for sign, r2 in handed:
+                            spot = NZ // 2 + sign * (reach + r2)
+                            to = along_z[sign * r2]
+                            src = block(z - sign * reach)
+                            send(src, to, sems[0].at[spot], sems[1].at[spot])
             elif n == 2:
-                arrived(block(z - sign * (reach + 1)), sems[1].at[reach])
+                for sign, r in handed:
+                    spot = NZ // 2 + sign * (reach + r)
+                    arrived(block(z - sign * (reach + r)), sems[1].at[spot])
                 self.ax.start(1)
                 self.share(0, 0)
             else:
@@ -290,15 +374,20 @@
         score_l[m, half] = value
         peak[m] = jnp.maximum(peak[m], lanes(value, jnp.maximum))
 
-    def near_values(m, half):
+    def add_values(m, part, stored, values):
+        top = peak[m, part]
+        parts = [
+            jnp.exp2(score[part, group(g)] * RATE - top)
+            for score in stored
+            for g in range(score.shape[1] // HDIM)
+        ]
+        weight = jnp.concatenate([one.astype(jnp.bfloat16) for one in parts], axis=1)
+        sums[m, part] += functools.reduce(jnp.add, parts)
+        acc[m, part] += jnp.dot(weight, values, preferred_element_type=jnp.float32)
+
+    def near_values(m, half, part):
         values = (prior[1] if half == 0 else own_v[...]).reshape(chunk, HDIM)
-        top = peak[m]
-        parts = [
-            jnp.exp2(score_l[m, half, :, group(g)] * RATE - top) for g in range(chunk // HDIM)
-        ]
-        weight = jnp.concatenate([part.astype(jnp.bfloat16) for part in parts], axis=1)
-        sums[m] += functools.reduce(jnp.add, parts)
-        acc[m] += jnp.dot(weight, values, preferred_element_type=jnp.float32)
+        add_values(m, part, [score_l.at[m, half]], values)
 
     def far_chunk(m, shift, pc):
         before_here = jnp.maximum((s - pc + NC) // NC - 1, 0)
@@ -325,45 +414,51 @@
 
         lax.fori_loop(0, NC, step, 0)
 
-    def far_values(m, pc):
-        store = (score_a, score_b)[m]
-
-        def step(shift, carry):
-            where, slot, _, size = far_chunk(m, shift, pc)
-            values = vert[(1, m) + where].reshape(size, HDIM)
-            top = peak[m]
-            parts = [
-                jnp.exp2(store[slot, :, group(g)] * RATE - top) for g in range(size // HDIM)
-            ]
-            weight = jnp.concatenate([part.astype(jnp.bfloat16) for part in parts], axis=1)
-            sums[m] += functools.reduce(jnp.add, parts)
-            acc[m] += jnp.dot(weight, values, preferred_element_type=jnp.float32)
+    def far_values(m, pc, part):
+        both = 1 if m == 0 else 2
+
+        def step(i, carry):
+            found = [far_chunk(m, i * both + k, pc) for k in range(both)]
+            values = [vert[(1, m) + where].reshape(size, HDIM) for where, _, _, size in found]
+            stored = [(score_a, score_b)[m].at[slot] for _, slot, _, _ in found]
+            add_values(m, part, stored, jnp.concatenate(values, axis=0))
             return carry
 
-        lax.fori_loop(0, (NX, NZ)[m], step, 0)
+        lax.fori_loop(0, (NX, NZ)[m] // both, step, 0)
 
     def set_top(m):
         top = jnp.max(peak[m], axis=1, keepdims=True) * RATE
         peak[m] = jnp.broadcast_to(top, (rows, HDIM))
 
-    stays = []
-
-    def finish(m):
-        total = jnp.sum(sums[m], axis=1, keepdims=True)
-        obuf[m] = (acc[m] / total).astype(jnp.bfloat16).reshape(ny, BLOCK, HDIM)
+
+    def finish(m, first, count):
+        part = slice(first * BLOCK, (first + count) * BLOCK)
+        total = jnp.sum(sums[m, part], axis=1, keepdims=True)
+        result = (acc[m, part] / total).astype(jnp.bfloat16)
+        obuf[m, first : first + count] = result.reshape(count, BLOCK, HDIM)
         my_col = pl.ds(pl.multiple_of((2 * j + m) * HDIM, HDIM), HDIM)
-        for r in order:
-            to = lax.rem(j + r, ny)
-            remote(
-                obuf.at[m, to],
-                out_ref.at[:, my_col],
-                (s, to),
-                out_send.at[m, to],
-                out_recv.at[m, j],
-            )
-        stay = pltpu.make_async_copy(obuf.at[m, j], out_ref.at[:, my_col], misc.at[7 + m])
-        stay.start()
-        stays.append(stay)
+        for to in range(first, first + count):
+
+            @pl.when(to != j)
+            def _():
+                out_copy(m, to, my_col).start()
+
+            @pl.when(to == j)
+            def _():
+                stay_copy(m, to, my_col).start()
+
+    def out_copy(m, to, my_col):
+        return pltpu.make_async_remote_copy(
+            obuf.at[m, to],
+            out_ref.at[:, my_col],
+            out_send.at[m, to],
+            out_recv.at[m, j],
+            device_id=(s, to),
+            device_id_type=MESH,
+        )
+
+    def stay_copy(m, to, my_col):
+        return pltpu.make_async_copy(obuf.at[m, to], out_ref.at[:, my_col], misc.at[7 + m])
 
     keys, values = Gather(0), Gather(1)
 
@@ -375,15 +470,13 @@
             keys.shared(m, shift)
             far_scores(m, shift)
 
-    def values_of(m):
-        far_values(m, core)
+    def take_shared(m):
         for t in range((NX, NZ)[m] // 2 + 1):
             for shift in far_shifts(t, (NX, NZ)[m]):
                 values.shared(m, shift)
-        far_values(m, 1 - core)
 
     for kind in range(2):
-        remote((k_ref, v_ref)[kind], raw.at[kind], (after, j), misc.at[3 + kind], misc.at[5 + kind])
+        start_prior(kind, True)
         y_start(kind)
     peak[...] = jnp.full(peak.shape, LOW, jnp.float32)
     sums[...] = jnp.zeros(sums.shape, jnp.float32)
@@ -396,49 +489,66 @@
     values.step(0)
     y_start(2)
     for kind in range(2):
-        arrived(raw.at[kind], misc.at[5 + kind])
-    y_start(3)
-    here.append(
-        pltpu.make_async_copy(raw.at[:, :, pl.ds(kv_col, HDIM)], prior.at[:, j], misc.at[9])
-    )
-    here[3].start()
+        start_prior(kind, False)
     set_near()
 
     half_x, half_z = NX // 2, NZ // 2
     steps = max(half_z + 1, half_x + 2)
-    work = [
-        (3, lambda: y_wait(2)),
-        (3, lambda: near_scores(1, 1)),
-        (3, lambda: scores_of(1, 0)),
-        (3, lambda: near_scores(0, 1)),
-    ]
-    for t in range(1, half_z + 1):
-        work.append((max(4, t + 2), lambda t=t: scores_of(1, t)))
-    for t in range(half_x + 1):
-        work.append((t + 4, lambda t=t: scores_of(0, t)))
-    work.append((steps, lambda: (y_wait(3), near_scores(1, 0), near_scores(0, 0))))
-    for n in range(1, steps + 1):
+    work = {
+        3: [lambda: y_wait(2), lambda: near_scores(1, 1), lambda: near_scores(0, 1)],
+        4: [lambda: scores_of(1, 0), lambda: scores_of(1, 1)],
+    }
+    for n in range(1, steps):
         keys.step(n)
         if n > 1:
             values.step(n - 1)
-        for due, unit in work:
-            if due == n or (n == steps and due > n):
+        else:
+            spread_prior()
+        if n in work:
+            for unit in work.pop(n):
                 unit()
+    values.step(steps - 1)
+    for n in sorted(work):
+        for unit in work[n]:
+            unit()
+    for t in range(half_x):
+        scores_of(0, t)
+    keys.step(steps)
+    scores_of(0, half_x)
+    take_prior()
+    near_scores(0, 0)
+    near_scores(1, 0)
+    every = slice(0, rows)
+    set_top(0)
+    near_values(0, 1, every)
+    near_values(0, 0, every)
     values.step(steps)
-    for m in (1, 0):
-        set_top(m)
-        near_values(m, 1)
-        near_values(m, 0)
-        values_of(m)
-        finish(m)
-
-    for m in (1, 0):
+    far_values(0, core, every)
+    take_shared(0)
+    far_values(0, 1 - core, every)
+    finish(0, 0, ny)
+    for t in range(2, half_z + 1):
+        scores_of(1, t)
+    set_top(1)
+    take_shared(1)
+    count = ny // 2
+    for first in (0, count):
+        part = slice(first * BLOCK, (first + count) * BLOCK)
+        near_values(1, 1, part)
+        near_values(1, 0, part)
+        for pc in range(NC):
+            far_values(1, pc, part)
+        finish(1, first, count)
+
+    for m in range(2):
+        my_col = pl.ds(pl.multiple_of((2 * j + m) * HDIM, HDIM), HDIM)
         for r in order:
             source = lax.rem(j + ny - r, ny)
             col = pl.ds(pl.multiple_of((2 * source + m) * HDIM, HDIM), HDIM)
             arrived(out_ref.at[:, col], out_recv.at[m, source])
-    for copy in stays:
-        copy.wait()
+            out_copy(m, lax.rem(j + r, ny), my_col).wait_send()
+        stay_copy(m, j, my_col).wait()
+    end_prior()
     for copy in sent:
         copy.wait_send()
 
@@ -479,8 +589,8 @@
             dma((2, 2, 2, half)),
             dma((2, NX - 1)),
             dma((2, NX - 1)),
-            dma((2, NZ - 1)),
-            dma((2, NZ - 1)),
+            dma((2, NZ + 1)),
+            dma((2, NZ + 1)),
             dma((2, nsib)),
             dma((2, nsib)),
             dma((10,)),

time: 66 us -> 66.3 us (level)
  the two profiles are of different devices: /device:TPU:1 before, /device:TPU:58 now
where the time goes in v2:
time: 66.3 us; the launch traced here: 66.2 us
  Pallas kernels  64.5 us (97%)
  local copies, waits for them, and re-layouts  1.67 us (3%)
    pallas_call x1, Pallas kernels, body(): pl.pallas_call(functools.partial(kernel, ny, ns), out_shape=jax.ShapeDtyp...  64.5 us
    unnamed x1, local copies, waits for them, and re-layouts  1.67 us

profile of v2, /device:TPU:58, one launch (start us, length us, event | category | flops | bytes accessed | tf_op | source)
XLA Modules:
  0.0 66.2 jit_solution(10119313709393215305)
XLA Ops:
  0.0 64.5 %shard_map.55 = bf16[64,2048]{1,0:T(8,128)(2,1)} custom-call(bf16[64,2048]{1,0:T(8,128)(2,1)} %q_ref.1, bf16[64,512]{1,0:T(8,128)(2,1)} %k_ref.1, bf16[64,512]{1,0:T(8,128)(2,1)} %v_ref.1, s32[16,64]{1,0:T(8,128)} %vert_ref.1, s32[5,16]{1,0:T(8,128)} %bitcast.1), custom_call_target="tpu_custom_call" | custom-call | tf_op jit(solution)/shard_map/pallas_call | solution.py:566
  64.5 1.7 %copy.7 = bf16[64,2048]{1,0:T(8,128)(2,1)} copy(bf16[64,2048]{1,0:T(8,128)(2,1)} %shard_map.55) | data formatting | bytes 524288

commit v3 on v2

--- a/solution.py
+++ b/solution.py
@@ -361,7 +361,7 @@
                 keep = keep | (dist == offs_ref[i, head])
             bias_l[m] = jnp.where(keep & (place >= least), 0.0, LOW)
 
-    def near_scores(m, half):
+    def near_scores(m, half, late=False):
         keys = (prior[0] if half == 0 else own_k[...]).reshape(chunk, HDIM)
         value = lax.dot_general(queries_of(m), keys, nt, preferred_element_type=jnp.float32)
         bias = bias_l[m, :, half * chunk : (half + 1) * chunk]
@@ -372,7 +372,16 @@
                 lax.broadcasted_iota(jnp.int32, (rows, chunk), 1) <= line, value, LOW
             )
         score_l[m, half] = value
-        peak[m] = jnp.maximum(peak[m], lanes(value, jnp.maximum))
+        best = lanes(value, jnp.maximum)
+        if late:
+            top = peak[m]
+            raised = jnp.maximum(top, jnp.max(best, axis=1, keepdims=True) * RATE)
+            factor = jnp.exp2(top - raised)
+            peak[m] = raised
+            sums[m] *= factor
+            acc[m] *= factor
+        else:
+            peak[m] = jnp.maximum(peak[m], best)
 
     def add_values(m, part, stored, values):
         top = peak[m, part]
@@ -515,20 +524,20 @@
         scores_of(0, t)
     keys.step(steps)
     scores_of(0, half_x)
-    take_prior()
-    near_scores(0, 0)
-    near_scores(1, 0)
     every = slice(0, rows)
     set_top(0)
     near_values(0, 1, every)
-    near_values(0, 0, every)
+    far_values(0, core, every)
     values.step(steps)
-    far_values(0, core, every)
     take_shared(0)
     far_values(0, 1 - core, every)
-    finish(0, 0, ny)
     for t in range(2, half_z + 1):
         scores_of(1, t)
+    take_prior()
+    near_scores(0, 0, late=True)
+    near_values(0, 0, every)
+    finish(0, 0, ny)
+    near_scores(1, 0)
     set_top(1)
     take_shared(1)
     count = ny // 2

time: 66.3 us -> 66.3 us (level)
  no operation moved by 1% of the time
where the time goes in v3:
time: 66.3 us; the launch traced here: 66.1 us
  Pallas kernels  64.4 us (97%)
  local copies, waits for them, and re-layouts  1.67 us (3%)
    pallas_call x1, Pallas kernels, body(): pl.pallas_call(functools.partial(kernel, ny, ns), out_shape=jax.ShapeDtyp...  64.4 us
    unnamed x1, local copies, waits for them, and re-layouts  1.67 us

profile of v3, /device:TPU:58, one launch (start us, length us, event | category | flops | bytes accessed | tf_op | source)
XLA Modules:
  0.0 66.1 jit_solution(9735425512461189984)
XLA Ops:
  0.0 64.4 %shard_map.55 = bf16[64,2048]{1,0:T(8,128)(2,1)} custom-call(bf16[64,2048]{1,0:T(8,128)(2,1)} %q_ref.1, bf16[64,512]{1,0:T(8,128)(2,1)} %k_ref.1, bf16[64,512]{1,0:T(8,128)(2,1)} %v_ref.1, s32[16,64]{1,0:T(8,128)} %vert_ref.1, s32[5,16]{1,0:T(8,128)} %bitcast.1), custom_call_target="tpu_custom_call" | custom-call | tf_op jit(solution)/shard_map/pallas_call | solution.py:575
  64.4 1.7 %copy.7 = bf16[64,2048]{1,0:T(8,128)(2,1)} copy(bf16[64,2048]{1,0:T(8,128)(2,1)} %shard_map.55) | data formatting | bytes 524288
